TPU v7x, 32 devices: a whole 2x2x4 slice. The times are simulated.
32 devices in a mesh: hours: 2 (over x), chan: 2 (over core), freq: 8 (over z, y).
Axes of the slice: x: 2, y: 2, z: 4, core: 2. Of those that a mesh axis runs over, the one named last changes fastest.
Arguments:
- samples: bfloat16 [1152, 32, 1024], P('chan', ('hours', 'freq')), parts along dimension 1, may hold values from -18 to 18
Outputs:
- cross_spectra: bfloat16 [2, 256, 1152, 1152], P(None, ('hours', 'freq'), None, 'chan'), parts along dimension 1
There are 2 independent parts, one for each index of `hours`. A program takes and returns all parts, laid end to end along the dimension named above; each array names one. Nothing has to cross between parts.
All inputs are finite; a program needn't handle non-finite values.
Results may differ from a plain program's by a relative error of at most 0.008.
Values may be sent and summed in bfloat16 or wider, within the bound.
A program may use at most 192 MiB of HBM per device.

v0:
```python
import math
import jax
import jax.numpy as jnp
from jax import lax
from jax.sharding import PartitionSpec as P

BINS = 128


def padded_2(cells, sides, width):
    for axis, dim in sides:
        count = lax.axis_size(axis)
        ends = count - 1
        head = lax.slice_in_dim(cells, 0, width, axis=dim)
        tail = lax.slice_in_dim(cells, cells.shape[dim] - width, cells.shape[dim], axis=dim)
        cells = jnp.concatenate(
            [
                lax.ppermute(tail, axis, [(i, (i + 1) % count) for i in range(ends)]),
                cells,
                lax.ppermute(head, axis, [((i + 1) % count, i) for i in range(ends)]),
            ],
            axis=dim,
        )
    return cells


def from_behind(value, axis, steps):
    count = lax.axis_size(axis)
    pairs = [(source, (source + steps) % count) for source in range(count)]
    return lax.ppermute(value, axis, pairs)


def bin_table(length, bins):
    position = lax.broadcasted_iota(jnp.int32, (length, bins), 0)
    number = lax.broadcasted_iota(jnp.int32, (length, bins), 1) + 1
    phase = (position * number % length).astype(jnp.float32) * (2.0 * math.pi / length)
    taper = 0.5 - 0.5 * jnp.cos(position.astype(jnp.float32) * (2.0 * math.pi / length))
    factor = math.sqrt(8.0 / (3.0 * length))
    table = jnp.concatenate([taper * jnp.cos(phase), -(taper * jnp.sin(phase))], axis=1) * factor
    return table.astype(jnp.bfloat16)


def whiten(padded, first_bin, total_bins):
    count_bins = padded.shape[1] - 4
    values = padded.astype(jnp.float32)
    power = values[0] * values[0] + values[1] * values[1]
    summed = power[0:count_bins] + power[1 : count_bins + 1]
    summed = summed + power[2 : count_bins + 2]
    summed = summed + power[3 : count_bins + 3]
    summed = summed + power[4 : count_bins + 4]
    which = first_bin + jnp.arange(count_bins, dtype=jnp.int32)
    upper = jnp.minimum(which + 2, total_bins - 1)
    lower = jnp.maximum(which - 2, 0)
    count = (upper - lower + 1).astype(jnp.float32)
    level = jnp.maximum(summed / count[:, None, None], 0.1)
    return (values[:, 2 : count_bins + 2] / jnp.sqrt(level)[None]).astype(jnp.bfloat16)


def local(samples):
    local_channels, local_windows, length = samples.shape
    table = bin_table(length, BINS)
    spectrum = jnp.einsum("cws,sj->jwc", samples, table, preferred_element_type=jnp.float32)
    spectrum = spectrum.reshape(2, BINS, local_windows, local_channels).astype(jnp.bfloat16)
    arrived = lax.all_to_all(spectrum, "freq", split_axis=1, concat_axis=2, tiled=True)
    rimmed = padded_2(arrived, (("freq", 1),), 2)
    whitened = whiten(rimmed, lax.axis_index("freq") * arrived.shape[1], BINS)
    local_bins = whitened.shape[1]
    windows = whitened.shape[2]
    blocks = lax.axis_size("chan")
    own_block = lax.axis_index("chan")
    scale = 1.0 / windows
    visitors = [whitened]
    visiting = whitened
    visiting = from_behind(visiting, "chan", 1)
    visitors.append(visiting)
    stacked = jnp.stack(visitors)
    order = (own_block - jnp.arange(blocks, dtype=jnp.int32)) % blocks
    ordered = jnp.take(stacked, order, axis=0)
    every = jnp.transpose(ordered, (1, 2, 3, 0, 4)).reshape(
        2, local_bins, windows, blocks * local_channels
    )
    real_part = jnp.einsum("pkwb,pkwa->kba", every, whitened, preferred_element_type=jnp.float32)
    imag_part = jnp.einsum(
        "kwb,kwa->kba", every[0], whitened[1], preferred_element_type=jnp.float32
    )
    imag_part = imag_part - jnp.einsum(
        "kwb,kwa->kba", every[1], whitened[0], preferred_element_type=jnp.float32
    )
    return (jnp.stack([real_part, imag_part]) * scale).astype(jnp.bfloat16)


def solution(mesh):
    placed = (P("chan", ("hours", "freq"), None),)
    return jax.shard_map(
        local,
        mesh=mesh,
        in_specs=placed,
        out_specs=P(None, ("hours", "freq"), None, "chan"),
        check_vma=False,
    )
```

profile of v0, /device:TPU:0, one launch (start us, length us, event | category | flops | bytes accessed | tf_op | source)
XLA Modules:
  0.0 168.4 jit_solution(10404083622506896489)
XLA Ops:
  0.1 2.1 %cosine_multiply_fusion = (f32[1024,128]{1,0:T(8,128)S(1)}, f32[1024,128]{1,0:T(8,128)S(1)}) fusion(s32[128]{0:T(128)S(1)} %iota_add_fusion, f32[1024]{0:T(1024)S(1)} %multiply_subtract_fusion), kind=kLoop, calls=%fused_computation.36 | loop fusion | flops 2228224 | bytes 1053184 | tf_op jit(solution)/shard_map/mul | solution.py:39
  2.2 0.8 fusion.7
  3.0 0.1 convert_element_type.44
  3.1 2.7 %copy.14 = bf16[2,128,2,576]{3,2,0,1:T(2,128)(2,1)} copy(bf16[2,128,2,576]{1,0,3,2:T(2,128)(2,1)S(1)} %convert_element_type.44) | data formatting | bytes 1179648 | tf_op jit(solution)/shard_map/convert_element_type | solution.py:63
  5.8 7.3 %all-to-all-start = ((bf16[2,128,2,576]{3,2,0,1:T(2,128)(2,1)}), bf16[2,128,2,576]{3,2,0,1:T(2,128)(2,1)S(1)}, u32[]{:S(2)}, u32[]{:S(2)}) async-start(bf16[2,128,2,576]{3,2,0,1:T(2,128)(2,1)} %copy.14), calls=%async_computation | async-start | bytes 1310720 | tf_op jit(solution)/shard_map/all_to_all | solution.py:64
  13.1 17.3 %all-to-all-done = bf16[2,128,2,576]{3,2,0,1:T(2,128)(2,1)S(1)} async-done(((bf16[2,128,2,576]{3,2,0,1:T(2,128)(2,1)}), bf16[2,128,2,576]{3,2,0,1:T(2,128)(2,1)S(1)}, u32[]{:S(2)}, u32[]{:S(2)}) %all-to-all-start) | async-done | bytes 589856 | tf_op jit(solution)/shard_map/all_to_all | solution.py:64
  30.5 0.7 copy.16
  31.1 0.5 all_to_all.16
  31.7 3.4 %collective-permute-start = (bf16[2,2,16,576]{3,2,1,0:T(8,128)(2,1)S(1)}, bf16[2,2,16,576]{3,2,1,0:T(8,128)(2,1)S(1)}, u32[]{:S(2)}, u32[]{:S(2)}) collective-permute-start(bf16[2,2,16,576]{3,2,1,0:T(8,128)(2,1)S(1)} %get-tuple-element.7), channel_id=1, source_target_pairs={{0,1},{1,2},{2,3},{3,4},{4,5},{5,6},{6,7},{8,9},{9,10},{10,11},{11... | collective-permute-start | bytes 221192 | tf_op jit(solution)/shard_map/ppermute | solution.py:18
  35.1 1.3 collective-permute-start.1
  36.4 0.7 collective-permute-done
  37.1 4.3 %collective-permute-done.1 = bf16[2,2,16,576]{3,2,1,0:T(8,128)(2,1)S(1)} collective-permute-done((bf16[2,2,16,576]{3,2,1,0:T(8,128)(2,1)S(1)}, bf16[2,2,16,576]{3,2,1,0:T(8,128)(2,1)S(1)}, u32[]{:S(2)}, u32[]{:S(2)}) %collective-permute-start.1) | collective-permute-done | bytes 73760 | tf_op jit(solution)/shard_map/ppermute | solution.py:20
  41.4 0.2 maximum_convert_fusion
  41.6 0.1 fusion.11
  41.7 0.3 fusion.15
  42.0 0.1 fusion.6
  42.3 0.1 fusion.37
  42.4 1.9 %collective-permute-done.2 = bf16[2,16,16,576]{3,2,1,0:T(8,128)(2,1)S(1)} collective-permute-done((bf16[2,16,16,576]{3,2,1,0:T(8,128)(2,1)S(1)}, bf16[2,16,16,576]{3,2,1,0:T(8,128)(2,1)S(1)}, u32[]{:S(2)}, u32[]{:S(2)}) %collective-permute-start.2) | collective-permute-done | bytes 589856 | tf_op jit(solution)/shard_map/ppermute | solution.py:30
  44.3 0.2 pad_maximum_fusion
  44.5 1.8 %gather_fusion = bf16[2,2,16,16,576]{4,3,2,1,0:T(8,128)(2,1)} fusion(bf16[2,2,16,16,576]{4,3,2,1,0:T(8,128)(2,1)S(1)} %pad_maximum_fusion, s32[1024]{0:T(1024)S(1)} %pad_clamp_fusion), kind=kCustom, calls=%fused_computation | custom fusion | bytes 2359304 | tf_op jit(solution)/shard_map/jit(_take)/gather | solution.py:78
  46.3 1.5 select_bitcast_fusion
  47.8 2.4 %copy.17 = bf16[2,16,16,2,576]{4,3,2,1,0:T(2,128)(2,1)} copy(bf16[2,16,16,2,576]{4,2,1,0,3:T(8,128)(2,1)S(1)} %select_bitcast_fusion) | data formatting | bytes 2359296 | tf_op jit(solution)/shard_map/jit(_take)/select_n | solution.py:78
  50.2 1.0 fusion.31
  51.2 3.1 %reshape.85 = bf16[2,16,16,1152]{3,2,1,0:T(8,128)(2,1)S(1)} reshape(bf16[2,16,16,2,576]{4,3,2,1,0:T(2,128)(2,1)} %copy.17) | data formatting | bytes 2359296 | tf_op jit(solution)/shard_map/reshape | solution.py:79
  54.2 1.5 copy.19
  55.7 2.0 %squeeze.18 = bf16[16,16,1152]{2,1,0:T(8,128)(2,1)S(1)} reshape(bf16[1,16,16,2,576]{4,3,2,1,0:T(2,128)(2,1)} %copy.19) | data formatting | bytes 1179648 | tf_op jit(solution)/shard_map/squeeze | solution.py:87
  57.8 2.6 %copy.18 = bf16[1,16,16,2,576]{4,3,2,1,0:T(2,128)(2,1)} copy(bf16[1,16,16,2,576]{4,2,1,0,3:T(8,128)(2,1)} %get-tuple-element.6) | data formatting | bytes 1179648 | tf_op jit(solution)/shard_map/slice | solution.py:84
  60.4 2.0 %squeeze.16 = bf16[16,16,1152]{2,1,0:T(8,128)(2,1)S(1)} reshape(bf16[1,16,16,2,576]{4,3,2,1,0:T(2,128)(2,1)} %copy.18) | data formatting | bytes 1179648 | tf_op jit(solution)/shard_map/squeeze | solution.py:84
  62.4 16.5 %convolution_bitcast_fusion = f32[1,16,1152,576]{2,3,1,0:T(8,128)} fusion(bf16[2,16,16,1152]{3,2,1,0:T(8,128)(2,1)S(1)} %reshape.85, bf16[2,16,16,576]{3,2,1,0:T(8,128)(2,1)S(1)} %fusion.6), kind=kOutput, calls=%fused_computation.4 | convolution fusion | flops 679477248 | bytes 44236800 | tf_op jit(solution)/shard_map/pkwb,pkwa->kba/dot_general | solution.py:82
  78.9 17.6 %fusion.25 = f32[16,1152,576]{1,2,0:T(8,128)} fusion(bf16[16,16,1152]{2,1,0:T(8,128)(2,1)S(1)} %squeeze.16, bf16[2,16,16,576]{3,2,1,0:T(8,128)(2,1)S(1)} %fusion.6), kind=kOutput, calls=%fused_computation.42 | convolution fusion | flops 339738624 | bytes 43384832 | tf_op jit(solution)/shard_map/kwb,kwa->kba/dot_general | solution.py:83
  96.5 30.7 %subtract_bitcast_fusion = f32[1,16,1152,576]{2,3,1,0:T(8,128)} fusion(f32[16,1152,576]{1,2,0:T(8,128)} %fusion.25, bf16[16,16,1152]{2,1,0:T(8,128)(2,1)S(1)} %squeeze.18, bf16[2,16,16,576]{3,2,1,0:T(8,128)(2,1)S(1)} %fusion.6), kind=kOutput, calls=%fused_computation.3 | convolution fusion | flops 350355456 | bytes 85852160 | tf_op jit(solution)/shard_map/kwb,kwa->kba/dot_general | solution.py:86
  127.2 41.0 %fusion = bf16[2,16,1152,576]{2,3,1,0:T(8,128)(2,1)} fusion(f32[1,16,1152,576]{2,3,1,0:T(8,128)} %subtract_bitcast_fusion, f32[1,16,1152,576]{2,3,1,0:T(8,128)} %convolution_bitcast_fusion), kind=kLoop, calls=%fused_computation.2 | loop fusion | flops 63700992 | bytes 127401984 | tf_op jit(solution)/shard_map/convert_element_type | solution.py:89
  (13 shorter events, 0.3 us)
Async XLA Ops:
  0.0 2.2 %copy-start = (bf16[576,2,1024]{2,1,0:T(2,128)(2,1)S(1)}, bf16[576,2,1024]{2,1,0:T(2,128)(2,1)}, u32[]{:S(2)}) copy-start(bf16[576,2,1024]{2,1,0:T(2,128)(2,1)} %param.1) | copy-start | bytes 7077892
  5.8 24.6 %all-to-all-start = ((bf16[2,128,2,576]{3,2,0,1:T(2,128)(2,1)}), bf16[2,128,2,576]{3,2,0,1:T(2,128)(2,1)S(1)}, u32[]{:S(2)}, u32[]{:S(2)}) async-start(bf16[2,128,2,576]{3,2,0,1:T(2,128)(2,1)} %copy.14), calls=%async_computation | async-start | bytes 1310720 | tf_op jit(solution)/shard_map/all_to_all | solution.py:64
  31.7 5.4 %collective-permute-start = (bf16[2,2,16,576]{3,2,1,0:T(8,128)(2,1)S(1)}, bf16[2,2,16,576]{3,2,1,0:T(8,128)(2,1)S(1)}, u32[]{:S(2)}, u32[]{:S(2)}) collective-permute-start(bf16[2,2,16,576]{3,2,1,0:T(8,128)(2,1)S(1)} %get-tuple-element.7), channel_id=1, source_target_pairs={{0,1},{1,2},{2,3},{3,4},{4,5},{5,6},{6,7},{8,9},{9,10},{10,11},{11... | collective-permute-start | bytes 221192 | tf_op jit(solution)/shard_map/ppermute | solution.py:18
  35.1 6.3 %collective-permute-start.1 = (bf16[2,2,16,576]{3,2,1,0:T(8,128)(2,1)S(1)}, bf16[2,2,16,576]{3,2,1,0:T(8,128)(2,1)S(1)}, u32[]{:S(2)}, u32[]{:S(2)}) collective-permute-start(bf16[2,2,16,576]{3,2,1,0:T(8,128)(2,1)S(1)} %get-tuple-element.8), channel_id=1, source_target_pairs={{1,0},{2,1},{3,2},{4,3},{5,4},{6,5},{7,6},{9,8},{10,9},{11,10},{12... | collective-permute-start | bytes 221192 | tf_op jit(solution)/shard_map/ppermute | solution.py:20
  42.1 2.2 %collective-permute-start.2 = (bf16[2,16,16,576]{3,2,1,0:T(8,128)(2,1)S(1)}, bf16[2,16,16,576]{3,2,1,0:T(8,128)(2,1)S(1)}, u32[]{:S(2)}, u32[]{:S(2)}) collective-permute-start(bf16[2,16,16,576]{3,2,1,0:T(8,128)(2,1)S(1)} %fusion.6), channel_id=1, source_target_pairs={{0,8},{8,0},{1,9},{9,1},{2,10},{10,2},{3,11},{11,3},{4,12},{12,4},... | collective-permute-start | bytes 1769480 | tf_op jit(solution)/shard_map/ppermute | solution.py:30
  127.2 41.0 %copy-start.1 = (bf16[576,2,1024]{2,1,0:T(2,128)(2,1)S(1)}, bf16[576,2,1024]{2,1,0:T(2,128)(2,1)}, u32[]{:S(2)}) copy-start(bf16[576,2,1024]{2,1,0:T(2,128)(2,1)} %param.1) | copy-start | bytes 7077892
where the time goes:
time: 169 us; the launch traced here: 168 us
  matrix products  65.5 us (39%)
  other arithmetic  45.8 us (27%)
  waiting for transfers between devices  24.2 us (14%)
  local copies, waits for them, and re-layouts  20.4 us (12%)
  starting transfers between devices  12 us (7%)
    convert_element_type x1, other arithmetic, local(): return (jnp.stack([real_part, imag_part]) * scale).astype(jnp.bfloat16)  41 us
    dot_general x1, matrix products, local(): jnp.einsum('kwb,kwa->kba', every[1], whitened[0], preferred_element_type=...  30.7 us
    dot_general x1, matrix products, local(): jnp.einsum('kwb,kwa->kba', every[0], whitened[1], preferred_element_type=...  17.6 us
    all_to_all x1, waiting for transfers between devices, local(): lax.all_to_all(spectrum, 'freq', split_axis=1, concat_axis=2, tiled=True)  17.3 us
    dot_general x1, matrix products, local(): jnp.einsum('pkwb,pkwa->kba', every, whitened, preferred_element_type=jnp....  16.5 us
    all_to_all x1, starting transfers between devices, local(): lax.all_to_all(spectrum, 'freq', split_axis=1, concat_axis=2, tiled=True)  7.28 us
    ppermute x1, waiting for transfers between devices, padded_2(): lax.ppermute(head, axis, [((i + 1) % count, i) for i in range(ends)])  4.3 us
  transfers between devices with their start and end apart: 4, of which 4 were waited for; matrix products, arithmetic and copies ran while one was open for 0% of the time, Pallas kernels for 0%

commit v1 on v0

--- a/solution.py
+++ b/solution.py
@@ -5,6 +5,17 @@
 from jax.sharding import PartitionSpec as P
 
 BINS = 128
+
+
+def yards_wrap(obj, where_dim, message):
+    piece_now, all_values = (obj.shape[:where_dim], obj.shape[where_dim + 1 :])
+    return jnp.moveaxis(obj.reshape(*piece_now, message, -1, *all_values), where_dim, 0)
+
+
+def slabs_wait(array_in, out_dim):
+    top = list(array_in.shape[1:])
+    top[out_dim] *= array_in.shape[0]
+    return jnp.moveaxis(array_in, 0, out_dim).reshape(top)
 
 
 def padded_2(cells, sides, width):
@@ -61,7 +72,18 @@
     table = bin_table(length, BINS)
     spectrum = jnp.einsum("cws,sj->jwc", samples, table, preferred_element_type=jnp.float32)
     spectrum = spectrum.reshape(2, BINS, local_windows, local_channels).astype(jnp.bfloat16)
-    arrived = lax.all_to_all(spectrum, "freq", split_axis=1, concat_axis=2, tiled=True)
+    high, spare = (lax.psum(1, axis_name="freq"), lax.axis_index("freq"))
+    right_arr = yards_wrap(spectrum, 1, high)
+    all_blocks = [right_arr[spare]]
+    j0 = 1
+    while j0 < high:
+        x_new = right_arr[(spare + j0) % high]
+        all_blocks.append(
+            lax.ppermute(x_new, "freq", perm=[(h, (h + j0) % high) for h in range(high)])
+        )
+        j0 += 1
+    right_arr = jnp.stack(all_blocks)[(spare - jnp.arange(high)) % high]
+    arrived = slabs_wait(right_arr, 2)
     rimmed = padded_2(arrived, (("freq", 1),), 2)
     whitened = whiten(rimmed, lax.axis_index("freq") * arrived.shape[1], BINS)
     local_bins = whitened.shape[1]

time: 169 us -> 162 us (0.959)
  waiting for transfers between devices: 24.2 us -> 11.4 us
  starting transfers between devices: 12 us -> 19.7 us
  local copies, waits for them, and re-layouts: 20.4 us -> 18.6 us
    all_to_all x1 -> x0, waiting for transfers between devices: 17.3 us -> none  [local(): lax.all_to_all(spectrum, 'freq', split_axis=1, concat_axis=2, tiled=True)]
    ppermute x0 -> x7, starting transfers between devices: none -> 14.1 us  [local(): lax.ppermute(x_new, 'freq', perm=[(h, (h + j0) % high) for h in range(hig...]
    all_to_all x1 -> x0, starting transfers between devices: 7.28 us -> none  [local(): lax.all_to_all(spectrum, 'freq', split_axis=1, concat_axis=2, tiled=True)]
    ppermute x0 -> x7, waiting for transfers between devices: none -> 4.5 us  [local(): lax.ppermute(x_new, 'freq', perm=[(h, (h + j0) % high) for h in range(hig...]
    convert_element_type x2 -> x1, local copies, waits for them, and re-layouts: 2.82 us -> 0.29 us  [local(): spectrum.reshape(2, BINS, local_windows, local_channels)]
  transfers between devices with their start and end apart: 4 -> 10, of which waited for: 4 -> 6; matrix products, arithmetic and copies ran while one was open for 0% -> 0% of each run, Pallas kernels for 0% -> 0%
where the time goes in v1:
time: 162 us
  matrix products  65.5 us (40%)
  other arithmetic  45.9 us (28%)
  starting transfers between devices  19.7 us (12%)
  local copies, waits for them, and re-layouts  18.6 us (11%)
  waiting for transfers between devices  11.4 us (7%)
    convert_element_type x1, other arithmetic, local(): return (jnp.stack([real_part, imag_part]) * scale).astype(jnp.bfloat16)  41 us
    dot_general x1, matrix products, local(): jnp.einsum('kwb,kwa->kba', every[1], whitened[0], preferred_element_type=...  30.7 us
    dot_general x1, matrix products, local(): jnp.einsum('kwb,kwa->kba', every[0], whitened[1], preferred_element_type=...  17.6 us
    dot_general x1, matrix products, local(): jnp.einsum('pkwb,pkwa->kba', every, whitened, preferred_element_type=jnp....  16.5 us
    ppermute x7, starting transfers between devices, local(): lax.ppermute(x_new, 'freq', perm=[(h, (h + j0) % high) for h in range(hig...  14.1 us
    ppermute x7, waiting for transfers between devices, local(): lax.ppermute(x_new, 'freq', perm=[(h, (h + j0) % high) for h in range(hig...  4.5 us
    ppermute x1, waiting for transfers between devices, padded_2(): lax.ppermute(head, axis, [((i + 1) % count, i) for i in range(ends)])  4.3 us
    ppermute x1, starting transfers between devices, padded_2(): lax.ppermute(tail, axis, [(i, (i + 1) % count) for i in range(ends)])  4.22 us
  transfers between devices with their start and end apart: 10, of which 6 were waited for; matrix products, arithmetic and copies ran while one was open for 0% of the time, Pallas kernels for 0%

profile of v1, /device:TPU:0, one launch (start us, length us, event | category | flops | bytes accessed | tf_op | source)
XLA Modules:
  0.0 161.5 jit_solution(14397242577792959609)
XLA Ops:
  0.1 2.1 %cosine_multiply_fusion = (f32[1024,128]{1,0:T(8,128)S(1)}, f32[1024,128]{1,0:T(8,128)S(1)}) fusion(s32[128]{0:T(128)S(1)} %iota_add_fusion, f32[1024]{0:T(1024)S(1)} %multiply_subtract_fusion), kind=kLoop, calls=%fused_computation.37 | loop fusion | flops 2228224 | bytes 1053184 | tf_op jit(solution)/shard_map/mul | solution.py:50
  2.2 0.8 fusion.7
  3.4 3.0 %collective-permute-start = (bf16[2,16,2,576]{3,1,2,0:T(8,128)(2,1)S(1)}, bf16[2,16,2,576]{3,1,2,0:T(8,128)(2,1)S(1)}, u32[]{:S(2)}, u32[]{:S(2)}) collective-permute-start(bf16[2,16,2,576]{3,1,2,0:T(8,128)(2,1)S(1)} %bitcast.84), channel_id=1, source_target_pairs={{0,1},{1,2},{2,3},{3,4},{4,5},{5,6},{6,7},{7,0},{8,9},{9,10},{10,1... | collective-permute-start | bytes 221192 | tf_op jit(solution)/shard_map/ppermute | solution.py:82
  6.5 1.6 %collective-permute-start.1 = (bf16[2,16,2,576]{3,1,2,0:T(8,128)(2,1)S(1)}, bf16[2,16,2,576]{3,1,2,0:T(8,128)(2,1)S(1)}, u32[]{:S(2)}, u32[]{:S(2)}) collective-permute-start(bf16[2,16,2,576]{3,1,2,0:T(8,128)(2,1)S(1)} %bitcast.83), channel_id=1, source_target_pairs={{0,2},{1,3},{2,4},{3,5},{4,6},{5,7},{6,0},{7,1},{8,10},{9,11},{10,... | collective-permute-start | bytes 221192 | tf_op jit(solution)/shard_map/ppermute | solution.py:82
  8.1 2.6 %collective-permute-start.2 = (bf16[2,16,2,576]{3,1,2,0:T(8,128)(2,1)S(1)}, bf16[2,16,2,576]{3,1,2,0:T(8,128)(2,1)S(1)}, u32[]{:S(2)}, u32[]{:S(2)}) collective-permute-start(bf16[2,16,2,576]{3,1,2,0:T(8,128)(2,1)S(1)} %bitcast.81), channel_id=1, source_target_pairs={{0,3},{1,4},{2,5},{3,6},{4,7},{5,0},{6,1},{7,2},{8,11},{9,12},{10,... | collective-permute-start | bytes 221192 | tf_op jit(solution)/shard_map/ppermute | solution.py:82
  10.7 1.3 collective-permute-start.3
  12.0 2.7 %collective-permute-start.4 = (bf16[2,16,2,576]{3,1,2,0:T(8,128)(2,1)S(1)}, bf16[2,16,2,576]{3,1,2,0:T(8,128)(2,1)S(1)}, u32[]{:S(2)}, u32[]{:S(2)}) collective-permute-start(bf16[2,16,2,576]{3,1,2,0:T(8,128)(2,1)S(1)} %bitcast.79), channel_id=1, source_target_pairs={{0,5},{1,6},{2,7},{3,0},{4,1},{5,2},{6,3},{7,4},{8,13},{9,14},{10,... | collective-permute-start | bytes 221192 | tf_op jit(solution)/shard_map/ppermute | solution.py:82
  14.8 1.4 collective-permute-start.5
  16.2 1.5 collective-permute-start.6
  17.7 1.5 collective-permute-done.2
  19.2 0.7 collective-permute-done.3
  19.9 2.3 %collective-permute-done.5 = bf16[2,16,2,576]{3,1,2,0:T(8,128)(2,1)S(1)} collective-permute-done((bf16[2,16,2,576]{3,1,2,0:T(8,128)(2,1)S(1)}, bf16[2,16,2,576]{3,1,2,0:T(8,128)(2,1)S(1)}, u32[]{:S(2)}, u32[]{:S(2)}) %collective-permute-start.5) | collective-permute-done | bytes 73760 | tf_op jit(solution)/shard_map/ppermute | solution.py:82
  22.3 0.7 gather_fusion
  23.5 0.5 reshape.154
  24.0 4.2 %collective-permute-start.7 = (bf16[2,2,16,576]{3,2,1,0:T(8,128)(2,1)S(1)}, bf16[2,2,16,576]{3,2,1,0:T(8,128)(2,1)S(1)}, u32[]{:S(2)}, u32[]{:S(2)}) collective-permute-start(bf16[2,2,16,576]{3,2,1,0:T(8,128)(2,1)S(1)} %get-tuple-element.7), channel_id=1, source_target_pairs={{0,1},{1,2},{2,3},{3,4},{4,5},{5,6},{6,7},{8,9},{9,10},{10,11},{11... | collective-permute-start | bytes 221192 | tf_op jit(solution)/shard_map/ppermute | solution.py:29
  28.2 1.3 collective-permute-start.8
  29.6 0.7 collective-permute-done.7
  30.3 4.3 %collective-permute-done.8 = bf16[2,2,16,576]{3,2,1,0:T(8,128)(2,1)S(1)} collective-permute-done((bf16[2,2,16,576]{3,2,1,0:T(8,128)(2,1)S(1)}, bf16[2,2,16,576]{3,2,1,0:T(8,128)(2,1)S(1)}, u32[]{:S(2)}, u32[]{:S(2)}) %collective-permute-start.8) | collective-permute-done | bytes 73760 | tf_op jit(solution)/shard_map/ppermute | solution.py:31
  35.6 1.9 %collective-permute-done.9 = bf16[2,16,16,576]{3,2,1,0:T(8,128)(2,1)S(1)} collective-permute-done((bf16[2,16,16,576]{3,2,1,0:T(8,128)(2,1)S(1)}, bf16[2,16,16,576]{3,2,1,0:T(8,128)(2,1)S(1)}, u32[]{:S(2)}, u32[]{:S(2)}) %collective-permute-start.9) | collective-permute-done | bytes 589856 | tf_op jit(solution)/shard_map/ppermute | solution.py:41
  37.7 1.8 %gather_fusion.1 = bf16[2,2,16,16,576]{4,3,2,1,0:T(8,128)(2,1)} fusion(bf16[2,2,16,16,576]{4,3,2,1,0:T(8,128)(2,1)S(1)} %pad_maximum_fusion, s32[1024]{0:T(1024)S(1)} %pad_clamp_fusion), kind=kCustom, calls=%fused_computation.1 | custom fusion | bytes 2359304 | tf_op jit(solution)/shard_map/jit(_take)/gather | solution.py:100
  39.5 1.5 select_bitcast_fusion
  41.0 2.4 %copy.15 = bf16[2,16,16,2,576]{4,3,2,1,0:T(2,128)(2,1)} copy(bf16[2,16,16,2,576]{4,2,1,0,3:T(8,128)(2,1)S(1)} %select_bitcast_fusion) | data formatting | bytes 2359296 | tf_op jit(solution)/shard_map/jit(_take)/select_n | solution.py:100
  43.4 1.0 fusion.33
  44.3 3.1 %reshape.177 = bf16[2,16,16,1152]{3,2,1,0:T(8,128)(2,1)S(1)} reshape(bf16[2,16,16,2,576]{4,3,2,1,0:T(2,128)(2,1)} %copy.15) | data formatting | bytes 2359296 | tf_op jit(solution)/shard_map/reshape | solution.py:101
  47.4 1.5 copy.19
  48.9 2.0 %squeeze.46 = bf16[16,16,1152]{2,1,0:T(8,128)(2,1)S(1)} reshape(bf16[1,16,16,2,576]{4,3,2,1,0:T(2,128)(2,1)} %copy.19) | data formatting | bytes 1179648 | tf_op jit(solution)/shard_map/squeeze | solution.py:109
  51.0 2.6 %copy.18 = bf16[1,16,16,2,576]{4,3,2,1,0:T(2,128)(2,1)} copy(bf16[1,16,16,2,576]{4,2,1,0,3:T(8,128)(2,1)} %get-tuple-element.6) | data formatting | bytes 1179648 | tf_op jit(solution)/shard_map/slice | solution.py:106
  53.6 2.0 %squeeze.44 = bf16[16,16,1152]{2,1,0:T(8,128)(2,1)S(1)} reshape(bf16[1,16,16,2,576]{4,3,2,1,0:T(2,128)(2,1)} %copy.18) | data formatting | bytes 1179648 | tf_op jit(solution)/shard_map/squeeze | solution.py:106
  55.6 16.5 %convolution_bitcast_fusion = f32[1,16,1152,576]{2,3,1,0:T(8,128)} fusion(bf16[2,16,16,1152]{3,2,1,0:T(8,128)(2,1)S(1)} %reshape.177, bf16[2,16,16,576]{3,2,1,0:T(8,128)(2,1)S(1)} %fusion.6), kind=kOutput, calls=%fused_computation.5 | convolution fusion | flops 679477248 | bytes 44236800 | tf_op jit(solution)/shard_map/pkwb,pkwa->kba/dot_general | solution.py:104
  72.1 17.6 %fusion.25 = f32[16,1152,576]{1,2,0:T(8,128)} fusion(bf16[16,16,1152]{2,1,0:T(8,128)(2,1)S(1)} %squeeze.44, bf16[2,16,16,576]{3,2,1,0:T(8,128)(2,1)S(1)} %fusion.6), kind=kOutput, calls=%fused_computation.43 | convolution fusion | flops 339738624 | bytes 43384832 | tf_op jit(solution)/shard_map/kwb,kwa->kba/dot_general | solution.py:105
  89.7 30.7 %subtract_bitcast_fusion = f32[1,16,1152,576]{2,3,1,0:T(8,128)} fusion(f32[16,1152,576]{1,2,0:T(8,128)} %fusion.25, bf16[16,16,1152]{2,1,0:T(8,128)(2,1)S(1)} %squeeze.46, bf16[2,16,16,576]{3,2,1,0:T(8,128)(2,1)S(1)} %fusion.6), kind=kOutput, calls=%fused_computation.4 | convolution fusion | flops 350355456 | bytes 85852160 | tf_op jit(solution)/shard_map/kwb,kwa->kba/dot_general | solution.py:108
  120.3 41.0 %fusion = bf16[2,16,1152,576]{2,3,1,0:T(8,128)(2,1)} fusion(f32[1,16,1152,576]{2,3,1,0:T(8,128)} %subtract_bitcast_fusion, f32[1,16,1152,576]{2,3,1,0:T(8,128)} %convolution_bitcast_fusion), kind=kLoop, calls=%fused_computation.3 | loop fusion | flops 63700992 | bytes 127401984 | tf_op jit(solution)/shard_map/convert_element_type | solution.py:111
  (42 shorter events, 2.3 us)
Async XLA Ops:
  0.0 2.2 %copy-start = (bf16[576,2,1024]{2,1,0:T(2,128)(2,1)S(1)}, bf16[576,2,1024]{2,1,0:T(2,128)(2,1)}, u32[]{:S(2)}) copy-start(bf16[576,2,1024]{2,1,0:T(2,128)(2,1)} %param.1) | copy-start | bytes 7077892
  3.4 11.4 %collective-permute-start = (bf16[2,16,2,576]{3,1,2,0:T(8,128)(2,1)S(1)}, bf16[2,16,2,576]{3,1,2,0:T(8,128)(2,1)S(1)}, u32[]{:S(2)}, u32[]{:S(2)}) collective-permute-start(bf16[2,16,2,576]{3,1,2,0:T(8,128)(2,1)S(1)} %bitcast.84), channel_id=1, source_target_pairs={{0,1},{1,2},{2,3},{3,4},{4,5},{5,6},{6,7},{7,0},{8,9},{9,10},{10,1... | collective-permute-start | bytes 221192 | tf_op jit(solution)/shard_map/ppermute | solution.py:82
  6.5 9.8 %collective-permute-start.1 = (bf16[2,16,2,576]{3,1,2,0:T(8,128)(2,1)S(1)}, bf16[2,16,2,576]{3,1,2,0:T(8,128)(2,1)S(1)}, u32[]{:S(2)}, u32[]{:S(2)}) collective-permute-start(bf16[2,16,2,576]{3,1,2,0:T(8,128)(2,1)S(1)} %bitcast.83), channel_id=1, source_target_pairs={{0,2},{1,3},{2,4},{3,5},{4,6},{5,7},{6,0},{7,1},{8,10},{9,11},{10,... | collective-permute-start | bytes 221192 | tf_op jit(solution)/shard_map/ppermute | solution.py:82
  8.1 11.1 %collective-permute-start.2 = (bf16[2,16,2,576]{3,1,2,0:T(8,128)(2,1)S(1)}, bf16[2,16,2,576]{3,1,2,0:T(8,128)(2,1)S(1)}, u32[]{:S(2)}, u32[]{:S(2)}) collective-permute-start(bf16[2,16,2,576]{3,1,2,0:T(8,128)(2,1)S(1)} %bitcast.81), channel_id=1, source_target_pairs={{0,3},{1,4},{2,5},{3,6},{4,7},{5,0},{6,1},{7,2},{8,11},{9,12},{10,... | collective-permute-start | bytes 221192 | tf_op jit(solution)/shard_map/ppermute | solution.py:82
  10.7 9.2 %collective-permute-start.3 = (bf16[2,16,2,576]{3,1,2,0:T(8,128)(2,1)S(1)}, bf16[2,16,2,576]{3,1,2,0:T(8,128)(2,1)S(1)}, u32[]{:S(2)}, u32[]{:S(2)}) collective-permute-start(bf16[2,16,2,576]{3,1,2,0:T(8,128)(2,1)S(1)} %bitcast.80), channel_id=1, source_target_pairs={{0,4},{1,5},{2,6},{3,7},{4,0},{5,1},{6,2},{7,3},{8,12},{9,13},{10,... | collective-permute-start | bytes 221192 | tf_op jit(solution)/shard_map/ppermute | solution.py:82
  12.0 7.9 %collective-permute-start.4 = (bf16[2,16,2,576]{3,1,2,0:T(8,128)(2,1)S(1)}, bf16[2,16,2,576]{3,1,2,0:T(8,128)(2,1)S(1)}, u32[]{:S(2)}, u32[]{:S(2)}) collective-permute-start(bf16[2,16,2,576]{3,1,2,0:T(8,128)(2,1)S(1)} %bitcast.79), channel_id=1, source_target_pairs={{0,5},{1,6},{2,7},{3,0},{4,1},{5,2},{6,3},{7,4},{8,13},{9,14},{10,... | collective-permute-start | bytes 221192 | tf_op jit(solution)/shard_map/ppermute | solution.py:82
  14.8 7.5 %collective-permute-start.5 = (bf16[2,16,2,576]{3,1,2,0:T(8,128)(2,1)S(1)}, bf16[2,16,2,576]{3,1,2,0:T(8,128)(2,1)S(1)}, u32[]{:S(2)}, u32[]{:S(2)}) collective-permute-start(bf16[2,16,2,576]{3,1,2,0:T(8,128)(2,1)S(1)} %bitcast.85), channel_id=1, source_target_pairs={{0,6},{1,7},{2,0},{3,1},{4,2},{5,3},{6,4},{7,5},{8,14},{9,15},{10,... | collective-permute-start | bytes 221192 | tf_op jit(solution)/shard_map/ppermute | solution.py:82
  16.2 6.0 %collective-permute-start.6 = (bf16[2,16,2,576]{3,1,2,0:T(8,128)(2,1)S(1)}, bf16[2,16,2,576]{3,1,2,0:T(8,128)(2,1)S(1)}, u32[]{:S(2)}, u32[]{:S(2)}) collective-permute-start(bf16[2,16,2,576]{3,1,2,0:T(8,128)(2,1)S(1)} %bitcast.82), channel_id=1, source_target_pairs={{0,7},{1,0},{2,1},{3,2},{4,3},{5,4},{6,5},{7,6},{8,15},{9,8},{10,9... | collective-permute-start | bytes 221192 | tf_op jit(solution)/shard_map/ppermute | solution.py:82
  24.0 6.3 %collective-permute-start.7 = (bf16[2,2,16,576]{3,2,1,0:T(8,128)(2,1)S(1)}, bf16[2,2,16,576]{3,2,1,0:T(8,128)(2,1)S(1)}, u32[]{:S(2)}, u32[]{:S(2)}) collective-permute-start(bf16[2,2,16,576]{3,2,1,0:T(8,128)(2,1)S(1)} %get-tuple-element.7), channel_id=1, source_target_pairs={{0,1},{1,2},{2,3},{3,4},{4,5},{5,6},{6,7},{8,9},{9,10},{10,11},{11... | collective-permute-start | bytes 221192 | tf_op jit(solution)/shard_map/ppermute | solution.py:29
  28.2 6.3 %collective-permute-start.8 = (bf16[2,2,16,576]{3,2,1,0:T(8,128)(2,1)S(1)}, bf16[2,2,16,576]{3,2,1,0:T(8,128)(2,1)S(1)}, u32[]{:S(2)}, u32[]{:S(2)}) collective-permute-start(bf16[2,2,16,576]{3,2,1,0:T(8,128)(2,1)S(1)} %get-tuple-element.8), channel_id=1, source_target_pairs={{1,0},{2,1},{3,2},{4,3},{5,4},{6,5},{7,6},{9,8},{10,9},{11,10},{12... | collective-permute-start | bytes 221192 | tf_op jit(solution)/shard_map/ppermute | solution.py:31
  35.3 2.2 %collective-permute-start.9 = (bf16[2,16,16,576]{3,2,1,0:T(8,128)(2,1)S(1)}, bf16[2,16,16,576]{3,2,1,0:T(8,128)(2,1)S(1)}, u32[]{:S(2)}, u32[]{:S(2)}) collective-permute-start(bf16[2,16,16,576]{3,2,1,0:T(8,128)(2,1)S(1)} %fusion.6), channel_id=1, source_target_pairs={{0,8},{8,0},{1,9},{9,1},{2,10},{10,2},{3,11},{11,3},{4,12},{12,4},... | collective-permute-start | bytes 1769480 | tf_op jit(solution)/shard_map/ppermute | solution.py:41
  120.3 41.0 %copy-start.1 = (bf16[576,2,1024]{2,1,0:T(2,128)(2,1)S(1)}, bf16[576,2,1024]{2,1,0:T(2,128)(2,1)}, u32[]{:S(2)}) copy-start(bf16[576,2,1024]{2,1,0:T(2,128)(2,1)} %param.1) | copy-start | bytes 7077892
